TPU v7x, 128 devices: a whole 4x4x4 slice. The times are simulated.
128 devices in a mesh: blk: 4 (over x_lo, core), dom: 32 (over z, y, x_hi).
Axes of the slice: x: 4 (x_hi: 2, x_lo: 2; x = x_hi * 2 + x_lo), y: 4, z: 4, core: 2. Of those that a mesh axis runs over, the one named last changes fastest.
Arguments:
- node_feats: bfloat16 [65536, 512], P(('blk', 'dom')), may hold values from -6 to 6
- send_rows: int32 [128, 32, 32], P(('blk', 'dom')), may hold values from 0 to 511
- neighbour_slots: int32 [65536, 8], P(('blk', 'dom')), may hold values from 0 to 1535
- slot_mask: int32 [65536, 8], P(('blk', 'dom')), may hold values 0 or 1
- gate_weight: bfloat16 [512, 512], replicated, may hold values from -0.25 to 0.25
- source_weight: bfloat16 [512, 1024], replicated, may hold values from -0.25 to 0.25
- qkv_weight: bfloat16 [512, 1536], replicated, may hold values from -0.26516504 to 0.26516504
- out_weight: bfloat16 [512, 512], replicated, may hold values from -0.25 to 0.25
- cotangent: bfloat16 [65536, 512], P(('blk', 'dom')), may hold values from -6 to 6
Outputs:
- layer_out: bfloat16 [65536, 512], P(('blk', 'dom'))
- feats_grad: bfloat16 [65536, 512], P(('blk', 'dom'))
- gate_grad: float32 [512, 512], replicated
- source_grad: float32 [512, 1024], replicated
- qkv_grad: float32 [512, 1536], replicated
- out_grad: float32 [512, 512], replicated
Inputs may be any that keep to these rules, and one draw needn't show every extreme that they name: `send_rows`: local node indices of the sending device. `neighbour_slots`: rows below 512 are the device's own nodes, the others received rows.
All inputs are finite; a program needn't handle non-finite values. No bound on the sum of `slot_mask` on one device may be relied on, other than what follows from the above.
Results may differ from a plain program's by a relative error of at most 0.035.
Values may be sent and summed in bfloat16 or wider, within the bound.
No kernel may reach another device: no remote copies, remote signals or barrier semaphores. Data moves between devices by JAX's collectives and lax.ppermute only.
A program may use at most 256 MiB of HBM per device.

v0:
```python
import math
import jax
import jax.numpy as jnp
from jax import lax
from jax.sharding import PartitionSpec as P

HEADS = 8
HDIM = 64


def body(
    node_feats,
    send_rows,
    neighbour_slots,
    slot_mask,
    gate_weight,
    source_weight,
    qkv_weight,
    out_weight,
    cotangent,
):
    node_count, feat_width = node_feats.shape
    head_count = HEADS
    head_width = HDIM
    score_scale = 1.0 / math.sqrt(HDIM)
    peer_count = lax.axis_size("dom")
    outgoing = node_feats[send_rows[0]]
    incoming = lax.all_to_all(outgoing, "dom", split_axis=0, concat_axis=0, tiled=True)
    table = jnp.concatenate([node_feats, incoming.reshape(-1, feat_width)], axis=0)
    table_rows = table.shape[0]
    gate_term = jnp.dot(node_feats, gate_weight, preferred_element_type=jnp.float32)
    source_terms = jnp.dot(table, source_weight, preferred_element_type=jnp.float32)
    edge_source = source_terms[neighbour_slots]
    gate_open = jax.nn.sigmoid(gate_term[:, None, :] + edge_source[:, :, :feat_width])
    edge_value = edge_source[:, :, feat_width:]
    mask_float = slot_mask.astype(jnp.float32)
    slot_weight = mask_float / jnp.maximum(jnp.sum(mask_float, axis=1, keepdims=True), 1.0)
    message = jnp.sum(slot_weight[:, :, None] * gate_open * edge_value, axis=1)
    qkv = jnp.dot(node_feats, qkv_weight, preferred_element_type=jnp.float32).astype(jnp.bfloat16)
    queries = qkv[:, :feat_width].reshape(node_count, head_count, head_width)
    keys_vals = lax.all_gather(qkv[:, feat_width:], "blk", axis=0, tiled=True)
    seq_len = keys_vals.shape[0]
    all_keys = keys_vals[:, :feat_width].reshape(seq_len, head_count, head_width)
    all_values = keys_vals[:, feat_width:].reshape(seq_len, head_count, head_width)
    scores = (
        jnp.einsum("ihe,jhe->hij", queries, all_keys, preferred_element_type=jnp.float32)
        * score_scale
    )
    row_top = jnp.max(scores, axis=2, keepdims=True)
    raw_weights = jnp.exp(scores - row_top)
    row_total = jnp.sum(raw_weights, axis=2, keepdims=True)
    prob_weights = raw_weights / row_total
    prob_half = prob_weights.astype(jnp.bfloat16)
    mixed = (
        jnp.einsum("hij,jhe->ihe", prob_half, all_values, preferred_element_type=jnp.float32)
        .astype(jnp.bfloat16)
        .reshape(node_count, feat_width)
    )
    attended = jnp.dot(mixed, out_weight, preferred_element_type=jnp.float32)
    layer_out = (node_feats.astype(jnp.float32) + message + attended).astype(jnp.bfloat16)
    upstream = cotangent.astype(jnp.float32)
    grad_out_w = jnp.einsum("nd,ne->de", mixed, cotangent, preferred_element_type=jnp.float32)
    d_mixed = jnp.einsum(
        "ne,de->nd", cotangent, out_weight, preferred_element_type=jnp.float32
    ).astype(jnp.bfloat16)
    d_heads = d_mixed.reshape(node_count, head_count, head_width)
    row_delta = jnp.sum(
        d_heads.astype(jnp.float32)
        * mixed.reshape(node_count, head_count, head_width).astype(jnp.float32),
        axis=2,
    )
    d_probs = jnp.einsum("ihe,jhe->hij", d_heads, all_values, preferred_element_type=jnp.float32)
    d_scores = (prob_weights * (d_probs - row_delta.T[:, :, None]) * score_scale).astype(
        jnp.bfloat16
    )
    d_query = jnp.einsum(
        "hij,jhe->ihe", d_scores, all_keys, preferred_element_type=jnp.float32
    ).reshape(node_count, feat_width)
    count = node_count * lax.axis_size("blk")
    d_key = jnp.einsum("hij,ihe->jhe", d_scores, queries, preferred_element_type=jnp.float32)
    d_value = jnp.einsum("hij,ihe->jhe", prob_half, d_heads, preferred_element_type=jnp.float32)
    d_keyval = lax.psum_scatter(
        jnp.concatenate(
            [d_key.reshape(count, feat_width), d_value.reshape(count, feat_width)], axis=1
        ),
        "blk",
        scatter_dimension=0,
        tiled=True,
    )
    d_qkv = jnp.concatenate([d_query, d_keyval], axis=1).astype(jnp.bfloat16)
    grad_qkv_w = jnp.einsum("nd,nf->df", node_feats, d_qkv, preferred_element_type=jnp.float32)
    d_attn_input = jnp.einsum("nf,df->nd", d_qkv, qkv_weight, preferred_element_type=jnp.float32)
    edge_up = slot_weight[:, :, None] * upstream[:, None, :]
    d_edge_value = edge_up * gate_open
    d_edge_logit = edge_up * edge_value * gate_open * (1.0 - gate_open)
    d_gate = jnp.sum(d_edge_logit, axis=1).astype(jnp.bfloat16)
    edge_terms = jnp.concatenate([d_edge_logit, d_edge_value], axis=2).reshape(-1, 2 * feat_width)
    d_source = jax.ops.segment_sum(
        edge_terms, neighbour_slots.reshape(-1), num_segments=table_rows
    ).astype(jnp.bfloat16)
    grad_source_w = jnp.einsum("td,tf->df", table, d_source, preferred_element_type=jnp.float32)
    grad_gate_w = jnp.einsum("nd,nf->df", node_feats, d_gate, preferred_element_type=jnp.float32)
    d_table = jnp.einsum("tf,df->td", d_source, source_weight, preferred_element_type=jnp.float32)
    returned = lax.all_to_all(
        d_table[node_count:].reshape(peer_count, -1, feat_width).astype(jnp.bfloat16),
        "dom",
        split_axis=0,
        concat_axis=0,
        tiled=True,
    ).astype(jnp.float32)
    d_sent = jax.ops.segment_sum(
        returned.reshape(-1, feat_width), send_rows[0].reshape(-1), num_segments=node_count
    )
    d_gate_input = jnp.einsum("nf,df->nd", d_gate, gate_weight, preferred_element_type=jnp.float32)
    feats_grad = (upstream + d_attn_input + d_table[:node_count] + d_gate_input + d_sent).astype(
        jnp.bfloat16
    )
    weight_sums = lax.psum((grad_gate_w, grad_source_w, grad_qkv_w, grad_out_w), ("blk", "dom"))
    return (layer_out, feats_grad, weight_sums[0], weight_sums[1], weight_sums[2], weight_sums[3])


def solution(mesh):
    return jax.shard_map(
        body,
        mesh=mesh,
        in_specs=(
            P(("blk", "dom"), None),
            P(("blk", "dom"), None, None),
            P(("blk", "dom"), None),
            P(("blk", "dom"), None),
            P(),
            P(),
            P(),
            P(),
            P(("blk", "dom"), None),
        ),
        out_specs=(P(("blk", "dom"), None), P(("blk", "dom"), None), P(), P(), P(), P()),
        check_vma=False,
    )
```

profile of v0, /device:TPU:1, one launch (start us, length us, event | category | flops | bytes accessed | tf_op | source)
XLA Modules:
  0.0 508.1 jit_solution(13844792690348114465)
XLA Ops:
  7.2 0.0 all-gather.2.cloned.1.call-start
  7.2 1.3 copy-done
  8.6 2.0 convolution_convert_fusion
  10.6 1.1 copy-done.9
  11.8 1.1 slice.39
  12.8 0.0 all-gather.2.cloned.1.call-update
  12.9 0.0 reduce-scatter.2.cloned.1.call-start
  12.9 1.1 slice.41
  14.0 1.0 copy.27
  15.0 0.5 convolution_convert_fusion.1
  15.5 47.7 %all-gather.2.cloned.1.call-done = bf16[2048,1024]{1,0:T(8,128)(2,1)} async-done(((bf16[512,1024]{1,0:T(8,128)(2,1)}), bf16[2048,1024]{1,0:T(8,128)(2,1)}) %all-gather.2.cloned.1.call-update) | async-done | bytes 4194320 | tf_op jit(solution)/shard_map/all_gather | solution.py:41
  63.2 4.5 fusion.36
  67.7 4.0 copy.28
  71.7 3.9 copy.26
  75.6 16.6 %fusion.37 = (f32[8,512]{1,0:T(8,128)S(1)}, f32[8,512,2048]{2,1,0:T(8,128)}) fusion(bf16[512,8,64]{0,2,1:T(8,128)(2,1)S(1)} %bitcast.82, bf16[2048,8,64]{0,2,1:T(8,128)(2,1)} %bitcast.71), kind=kOutput, calls=%fused_computation.67 | convolution fusion | flops 1098909696 | bytes 36192256 | tf_op jit(solution)/shard_map/sub | solution.py:50
  92.2 19.0 %fusion.8 = bf16[8,512,2048]{2,1,0:T(8,128)(2,1)} fusion(f32[8,512,2048]{2,1,0:T(8,128)} %get-tuple-element.29, f32[8,512]{1,0:T(8,128)S(1)} %get-tuple-element.28), kind=kLoop, calls=%fused_computation.15 | loop fusion | flops 16777216 | bytes 50348032 | tf_op jit(solution)/shard_map/convert_element_type | solution.py:53
  111.3 13.0 %multiply_reduce_fusion.2 = (f32[512,8]{0,1:T(8,128)}, bf16[8,64,512]{2,1,0:T(8,128)(2,1)}) fusion(bf16[512,512]{0,1:T(8,128)(2,1)S(1)} %convolution_convert_fusion.1, bf16[2048,8,64]{0,2,1:T(8,128)(2,1)} %bitcast.73, bf16[8,512,2048]{2,1,0:T(8,128)(2,1)} %fusion.8), kind=kOutput, calls=%fused_computation.49 | convolution fusion | flops 1075048448 | bytes 19939328 | tf_op jit(solution)/shard_map/hij,jhe->ihe/dot_general | solution.py:55
  124.3 10.8 %fusion.40 = f32[8,64,2048]{2,1,0:T(8,128)} fusion(bf16[512,8,64]{0,2,1:T(8,128)(2,1)S(1)} %bitcast.77, bf16[8,512,2048]{2,1,0:T(8,128)(2,1)} %fusion.8), kind=kOutput, calls=%fused_computation.70 | convolution fusion | flops 1073741824 | bytes 21495808 | tf_op jit(solution)/shard_map/hij,ihe->jhe/dot_general | solution.py:81
  135.1 13.4 %multiply_convert_fusion = bf16[8,512,2048]{2,1,0:T(8,128)(2,1)S(1)} fusion(bf16[512,8,64]{0,2,1:T(8,128)(2,1)S(1)} %bitcast.78, bf16[2048,8,64]{0,2,1:T(8,128)(2,1)} %bitcast.74, f32[8,512]{1,0:T(8,128)} %bitcast.85, f32[8,512,2048]{2,1,0:T(8,128)} %get-tuple-element.29, f32[8,512]{1,0:T(8,128)S(1)} %get-tuple-element.28), kind=kOutput, calls=%fused_computation.5 | convolution fusion | flops 1115684864 | bytes 52985856 | tf_op jit(solution)/shard_map/ihe,jhe->hij/dot_general | solution.py:72
  148.5 7.0 %fusion.39 = f32[8,64,2048]{2,1,0:T(8,128)} fusion(bf16[512,8,64]{0,2,1:T(8,128)(2,1)} %bitcast.81, bf16[8,512,2048]{2,1,0:T(8,128)(2,1)S(1)} %multiply_convert_fusion), kind=kOutput, calls=%fused_computation.69 | convolution fusion | flops 1073741824 | bytes 21495808 | tf_op jit(solution)/shard_map/hij,ihe->jhe/dot_general | solution.py:80
  155.5 0.0 copy-done.2
  155.5 7.8 %pad_maximum_fusion = f32[2048,1024]{0,1:T(8,128)} fusion(f32[2048,512]{0,1:T(8,128)} %bitcast.69, f32[2048,512]{0,1:T(8,128)} %bitcast.70), kind=kLoop, calls=%fused_computation.25 | loop fusion | flops 2097152 | bytes 16777216 | tf_op jit(solution)/shard_map/concatenate | solution.py:83
  163.3 0.7 copy-done.14
  164.0 0.1 reshape.105
  164.1 0.3 copy-done.1
  164.3 5.1 gather_fusion
  169.4 9.2 %all-to-all-start = ((bf16[32,32,512]{2,1,0:T(8,128)(2,1)}), bf16[32,32,512]{2,1,0:T(8,128)(2,1)}, u32[]{:S(2)}, u32[]{:S(2)}) async-start(bf16[32,32,512]{2,1,0:T(8,128)(2,1)} %bitcast.79), calls=%async_computation | async-start | bytes 2097152 | tf_op jit(solution)/shard_map/all_to_all | solution.py:28
  178.7 0.2 all-reduce.3.cloned.1.call-start
  178.9 1.1 convert_element_type.58
  180.0 0.8 copy.29
  180.8 0.1 copy.25
  181.0 0.2 reshape.113
  181.2 0.1 copy.24
  181.3 1.1 reshape.121
  182.4 1.4 fusion.38
  183.8 25.8 %all-to-all-done = bf16[32,32,512]{2,1,0:T(8,128)(2,1)} async-done(((bf16[32,32,512]{2,1,0:T(8,128)(2,1)}), bf16[32,32,512]{2,1,0:T(8,128)(2,1)}, u32[]{:S(2)}, u32[]{:S(2)}) %all-to-all-start) | async-done | bytes 1048608 | tf_op jit(solution)/shard_map/all_to_all | solution.py:28
  209.6 6.0 %fusion.26 = f32[1536,1024]{1,0:T(8,128)} fusion(bf16[512,1024]{1,0:T(8,128)(2,1)} %param.14, bf16[1024,512]{1,0:T(8,128)(2,1)} %bitcast.2, bf16[512,512]{1,0:T(8,128)(2,1)S(1)} %copy-done.1), kind=kOutput, calls=%fused_computation.50 | convolution fusion | flops 1613758464 | bytes 8912896 | tf_op jit(solution)/shard_map/dot_general | solution.py:32
  215.6 25.1 %gather_fusion.1 = f32[4096,1024]{1,0:T(8,128)} fusion(f32[1536,1024]{1,0:T(8,128)} %fusion.26, s32[4096]{0:T(1024)S(1)} %broadcast_clamp_fusion), kind=kCustom, calls=%fused_computation.1 | custom fusion | bytes 33570816 | tf_op jit(solution)/shard_map/gather | solution.py:33
  240.7 18.9 %fusion.34 = (bf16[512,512]{1,0:T(8,128)(2,1)S(1)}, f32[512,8,512]{2,1,0:T(8,128)}, f32[512,8,512]{2,1,0:T(8,128)}, f32[512,512]{1,0:T(8,128)}) fusion(f32[512,8,1024]{2,1,0:T(8,128)} %bitcast.68, f32[512,512]{1,0:T(8,128)} %fusion.38, f32[512,512]{1,0:T(8,128)} %convert_element_type.58, f32[512,8]{1,0:T(8,128)S(1)} %copy.24), kind=kLoop, calls=%fused_computation.65 | loop fusion | flops 28835840 | bytes 37240832 | tf_op jit(solution)/shard_map/reduce_sum | solution.py:96
  259.6 38.4 %scatter_custom_fusion = f32[1536,1024]{1,0:T(8,128)} fusion(s32[4096]{0:T(1024)S(1)} %reshape.121, f32[512,8,512]{2,1,0:T(8,128)} %get-tuple-element.24, f32[]{:T(128)} %constant.2.clone.1, f32[512,8,512]{2,1,0:T(8,128)} %get-tuple-element.23, f32[]{:T(128)} %constant.7.clone.1), kind=kCustom, calls=%fused_computation.10 | custom fusion | flops 8388608 | bytes 23068680 | tf_op jit(solution)/shard_map/scatter-add | solution.py:98
  298.1 1.4 convolution_bitcast_fusion.1
  299.5 6.2 %fusion.20 = f32[512,1024]{1,0:T(8,128)} fusion(f32[1536,1024]{1,0:T(8,128)} %scatter_custom_fusion, bf16[1024,512]{1,0:T(8,128)(2,1)} %bitcast.2, bf16[512,512]{1,0:T(8,128)(2,1)S(1)} %copy-done.1), kind=kOutput, calls=%fused_computation.36 | convolution fusion | flops 1615331328 | bytes 9961472 | tf_op jit(solution)/shard_map/td,tf->df/dot_general | solution.py:101
  305.8 1.4 fusion.41
  307.2 12.4 %convolution_convert_fusion.2 = bf16[8,64,512]{2,1,0:T(8,128)(2,1)} fusion(bf16[2048,8,64]{0,2,1:T(8,128)(2,1)} %bitcast.72, bf16[8,512,2048]{2,1,0:T(8,128)(2,1)} %copy-done.2), kind=kOutput, calls=%fused_computation.47 | convolution fusion | flops 1074003968 | bytes 19398656 | tf_op jit(solution)/shard_map/hij,jhe->ihe/dot_general | solution.py:76
  319.6 1.7 convert.13
  321.4 1.0 copy-done.10
  322.3 3.7 convolution_bitcast_fusion
  326.0 0.0 all-reduce.3.cloned.1.call-update
  326.0 4.9 fusion.22
  331.0 1.7 copy-done.12
  332.6 1.1 slice.64
  333.8 4.9 all-to-all-start.1
  338.7 0.1 reshape.129
  338.8 2.9 fusion.25
  341.7 2.8 fusion.24
  344.5 1.4 convolution_add_fusion
  346.0 13.1 %all-to-all-done.1 = bf16[32,32,512]{2,1,0:T(8,128)(2,1)} async-done(((bf16[32,32,512]{2,1,0:T(8,128)(2,1)}), bf16[32,32,512]{2,1,0:T(8,128)(2,1)}, u32[]{:S(2)}, u32[]{:S(2)}) %all-to-all-start.1) | async-done | bytes 1048608 | tf_op jit(solution)/shard_map/all_to_all | solution.py:104
  359.0 9.4 %scatter_custom_fusion.1 = f32[512,512]{1,0:T(8,128)} fusion(f32[512,512]{1,0:T(8,128)} %convolution_add_fusion, s32[1024]{0:T(1024)S(1)} %reshape.129, bf16[1024,512]{1,0:T(8,128)(2,1)} %bitcast.26), kind=kCustom, calls=%fused_computation.32 | custom fusion | flops 1048576 | bytes 2097152 | tf_op jit(solution)/shard_map/scatter-add | solution.py:111
  368.4 2.1 convert_element_type.66
  370.6 120.5 %all-reduce.3.cloned.1.call-done = (f32[512,512]{0,1:T(8,128)}, f32[512,1024]{1,0:T(8,128)}, f32[512,1536]{0,1:T(8,128)}, f32[512,512]{1,0:T(8,128)}) async-done(((f32[512,512]{0,1:T(8,128)}, f32[512,1024]{1,0:T(8,128)}, f32[512,1536]{0,1:T(8,128)}, f32[512,512]{1,0:T(8,128)}), (f32[512,512]{0,1:T(8,128)}, f32[512,1024]{1,0:T(8,128)}, f32[512,1536]{0,1:T(8,128)}, ...) | async-done | bytes 7340048 | tf_op jit(solution)/shard_map/psum | solution.py:118
  491.0 2.6 copy.30
  493.6 3.5 copy.31
  497.2 3.2 copy.37
  500.3 1.0 copy.38
  (34 shorter events, 0.1 us)
Async XLA Ops:
  7.2 1.4 copy-start
  7.2 7.8 %copy-start.3 = (bf16[512,512]{1,0:T(8,128)(2,1)S(1)}, bf16[512,512]{1,0:T(8,128)(2,1)}, u32[]{:S(2)}) copy-start(bf16[512,512]{1,0:T(8,128)(2,1)} %param.17) | copy-start | bytes 1572868
  7.2 7.8 %copy-start.5 = (bf16[512,512]{1,0:T(8,128)(2,1)S(1)}, bf16[512,512]{1,0:T(8,128)(2,1)}, u32[]{:S(2)}) copy-start(bf16[512,512]{1,0:T(8,128)(2,1)} %param.16) | copy-start | bytes 1572868
  7.2 56.0 %all-gather.2.cloned.1.call-start = ((), (), s32[]{:S(2)}) async-start(), calls=%async_computation.3 | async-start | bytes 5242880 | tf_op jit(solution)/shard_map/all_gather | solution.py:41
  10.6 1.1 copy-start.9
  12.9 306.7 %reduce-scatter.2.cloned.1.call-start = ((), (), s32[]{:S(2)}) async-start(), calls=%async_computation.4 | async-start | bytes 10485760 | tf_op jit(solution)/shard_map/reduce_scatter | solution.py:82
  67.7 7.9 %copy-start.8 = (bf16[512,512]{0,1:T(8,128)(2,1)S(1)}, bf16[512,512]{0,1:T(8,128)(2,1)}, u32[]{:S(2)}) copy-start(bf16[512,512]{0,1:T(8,128)(2,1)} %copy.27) | copy-start | bytes 1572868
  148.5 7.0 %copy-start.2 = (bf16[8,512,2048]{2,1,0:T(8,128)(2,1)}, bf16[8,512,2048]{2,1,0:T(8,128)(2,1)S(1)}, u32[]{:S(2)}) copy-start(bf16[8,512,2048]{2,1,0:T(8,128)(2,1)S(1)} %multiply_convert_fusion) | copy-start | bytes 50331652
  163.3 0.7 copy-start.14
  163.3 1.1 copy-start.1
  164.3 15.7 %copy-start.13 = (s32[512,8]{0,1:T(8,128)S(1)}, s32[512,8]{0,1:T(8,128)}, u32[]{:S(2)}) copy-start(s32[512,8]{0,1:T(8,128)} %param.11) | copy-start | bytes 49156
  164.3 16.8 %copy-start.15 = (s32[512,8]{0,1:T(8,128)S(1)}, s32[512,8]{0,1:T(8,128)}, u32[]{:S(2)}) copy-start(s32[512,8]{0,1:T(8,128)} %param.12) | copy-start | bytes 49156
  164.3 18.1 %copy-start.6 = (bf16[512,512]{1,0:T(8,128)(2,1)S(1)}, bf16[512,512]{1,0:T(8,128)(2,1)}, u32[]{:S(2)}) copy-start(bf16[512,512]{1,0:T(8,128)(2,1)} %param.13) | copy-start | bytes 1572868
  169.4 40.2 %all-to-all-start = ((bf16[32,32,512]{2,1,0:T(8,128)(2,1)}), bf16[32,32,512]{2,1,0:T(8,128)(2,1)}, u32[]{:S(2)}, u32[]{:S(2)}) async-start(bf16[32,32,512]{2,1,0:T(8,128)(2,1)} %bitcast.79), calls=%async_computation | async-start | bytes 2097152 | tf_op jit(solution)/shard_map/all_to_all | solution.py:28
  178.7 312.4 %all-reduce.3.cloned.1.call-start = ((), (), s32[]{:S(2)}) async-start(), calls=%async_computation.5 | async-start | bytes 14680064 | tf_op jit(solution)/shard_map/psum | solution.py:118
  298.1 7.7 %copy-start.4 = (bf16[8,64,512]{2,1,0:T(8,128)(2,1)S(1)}, bf16[8,64,512]{2,1,0:T(8,128)(2,1)}, u32[]{:S(2)}) copy-start(bf16[8,64,512]{2,1,0:T(8,128)(2,1)} %get-tuple-element.31) | copy-start | bytes 1572868
  321.3 1.0 copy-start.10
  331.0 1.7 copy-start.12
  333.8 25.3 %all-to-all-start.1 = ((bf16[32,32,512]{2,1,0:T(8,128)(2,1)}), bf16[32,32,512]{2,1,0:T(8,128)(2,1)}, u32[]{:S(2)}, u32[]{:S(2)}) async-start(bf16[32,32,512]{2,1,0:T(8,128)(2,1)} %bitcast.80), calls=%async_computation.2 | async-start | bytes 2097152 | tf_op jit(solution)/shard_map/all_to_all | solution.py:104
  338.8 5.7 %copy-start.7 = (bf16[512,512]{1,0:T(8,128)(2,1)S(1)}, bf16[512,512]{1,0:T(8,128)(2,1)}, u32[]{:S(2)}) copy-start(bf16[512,512]{1,0:T(8,128)(2,1)} %param.13) | copy-start | bytes 1572868
  491.0 9.3 %copy-start.11 = (f32[512,512]{1,0:T(8,128)S(1)}, f32[512,512]{1,0:T(8,128)}, u32[]{:S(2)}) copy-start(f32[512,512]{1,0:T(8,128)} %get-tuple-element.37) | copy-start | bytes 3145732
Sparse Core Ops, SparseCore 0:
  13.0 50.1 all-gather.1
  163.4 90.9 reduce-scatter.1
  326.2 164.8 all-reduce.2
where the time goes:
time: 515 us; the launch traced here: 508 us
  waiting for transfers between devices  207 us (40%)
  matrix products  108 us (21%)
  other arithmetic  98.5 us (19%)
  local copies, waits for them, and re-layouts  65.8 us (13%)
  starting transfers between devices  14.4 us (3%)
  between operations  14.2 us (3%)
    psum x1, waiting for transfers between devices, body(): lax.psum((grad_gate_w, grad_source_w, grad_qkv_w, grad_out_w), ('blk', 'd...  120 us
    all_gather x1, waiting for transfers between devices, body(): keys_vals = lax.all_gather(qkv[:, feat_width:], 'blk', axis=0, tiled=True)  47.7 us
    scatter-add x1, other arithmetic, body(): jax.ops.segment_sum(edge_terms, neighbour_slots.reshape(-1), num_segments...  38.4 us
    all_to_all x1, waiting for transfers between devices, body(): lax.all_to_all(outgoing, 'dom', split_axis=0, concat_axis=0, tiled=True)  25.8 us
    gather x1, local copies, waits for them, and re-layouts, body(): edge_source = source_terms[neighbour_slots]  25.1 us
    convert_element_type x1, other arithmetic, body(): prob_half = prob_weights.astype(jnp.bfloat16)  19 us
    reduce_sum x1, other arithmetic, body(): d_gate = jnp.sum(d_edge_logit, axis=1).astype(jnp.bfloat16)  18.9 us
    unnamed x37, local copies, waits for them, and re-layouts  17.2 us
  transfers between devices with their start and end apart: 5, of which 4 were waited for; matrix products, arithmetic and copies ran while one was open for 29% of the time, Pallas kernels for 0%

commit v1 on v0

--- a/solution.py
+++ b/solution.py
@@ -115,7 +115,9 @@
     feats_grad = (upstream + d_attn_input + d_table[:node_count] + d_gate_input + d_sent).astype(
         jnp.bfloat16
     )
-    weight_sums = lax.psum((grad_gate_w, grad_source_w, grad_qkv_w, grad_out_w), ("blk", "dom"))
+    weight_sums = lax.psum(
+        lax.psum((grad_gate_w, grad_source_w, grad_qkv_w, grad_out_w), "blk"), "dom"
+    )
     return (layer_out, feats_grad, weight_sums[0], weight_sums[1], weight_sums[2], weight_sums[3])
 
 

time: 515 us -> 908 us (1.76)
  the two profiles are of different devices: /device:TPU:1 before, /device:TPU:0 now
where the time goes in v1:
time: 908 us; the launch traced here: 901 us
  waiting for transfers between devices  595 us (66%)
  matrix products  108 us (12%)
  other arithmetic  98.7 us (11%)
  local copies, waits for them, and re-layouts  66 us (7%)
  starting transfers between devices  19.6 us (2%)
  between operations  14.3 us (2%)
    psum x1, waiting for transfers between devices, body(): lax.psum(lax.psum((grad_gate_w, grad_source_w, grad_qkv_w, grad_out_w), '...  360 us
    psum x1, waiting for transfers between devices, body(): lax.psum((grad_gate_w, grad_source_w, grad_qkv_w, grad_out_w), 'blk')  137 us
    all_gather x1, waiting for transfers between devices, body(): keys_vals = lax.all_gather(qkv[:, feat_width:], 'blk', axis=0, tiled=True)  46 us
    scatter-add x1, other arithmetic, body(): jax.ops.segment_sum(edge_terms, neighbour_slots.reshape(-1), num_segments...  38.4 us
    all_to_all x1, waiting for transfers between devices, body(): lax.all_to_all(outgoing, 'dom', split_axis=0, concat_axis=0, tiled=True)  26.6 us
    gather x1, local copies, waits for them, and re-layouts, body(): edge_source = source_terms[neighbour_slots]  25.3 us
    all_to_all x1, waiting for transfers between devices, body(): lax.all_to_all(d_table[node_count:].reshape(peer_count, -1, feat_width).a...  24.6 us
    reduce_sum x1, other arithmetic, body(): d_gate = jnp.sum(d_edge_logit, axis=1).astype(jnp.bfloat16)  19.1 us
  transfers between devices with their start and end apart: 6, of which 5 were waited for; matrix products, arithmetic and copies ran while one was open for 16% of the time, Pallas kernels for 0%

profile of v1, /device:TPU:0, one launch (start us, length us, event | category | flops | bytes accessed | tf_op | source)
XLA Modules:
  0.0 901.5 jit_solution(4384794739019038468)
XLA Ops:
  7.2 0.0 all-gather.2.cloned.1.call-start
  7.2 1.3 copy-done
  8.6 2.0 convolution_convert_fusion
  10.6 1.1 copy-done.9
  11.8 1.1 slice.39
  12.8 0.0 all-gather.2.cloned.1.call-update
  12.9 0.0 reduce-scatter.2.cloned.1.call-start
  12.9 1.1 slice.41
  14.0 1.0 copy.27
  15.0 0.5 convolution_convert_fusion.1
  15.5 46.0 %all-gather.2.cloned.1.call-done = bf16[2048,1024]{1,0:T(8,128)(2,1)} async-done(((bf16[512,1024]{1,0:T(8,128)(2,1)}), bf16[2048,1024]{1,0:T(8,128)(2,1)}) %all-gather.2.cloned.1.call-update) | async-done | bytes 4194320 | tf_op jit(solution)/shard_map/all_gather | solution.py:41
  61.5 4.5 fusion.36
  66.0 4.0 copy.28
  70.0 3.9 copy.26
  73.9 16.6 %fusion.37 = (f32[8,512]{1,0:T(8,128)S(1)}, f32[8,512,2048]{2,1,0:T(8,128)}) fusion(bf16[512,8,64]{0,2,1:T(8,128)(2,1)S(1)} %bitcast.82, bf16[2048,8,64]{0,2,1:T(8,128)(2,1)} %bitcast.71), kind=kOutput, calls=%fused_computation.67 | convolution fusion | flops 1098909696 | bytes 36192256 | tf_op jit(solution)/shard_map/sub | solution.py:50
  90.5 19.0 %fusion.8 = bf16[8,512,2048]{2,1,0:T(8,128)(2,1)} fusion(f32[8,512,2048]{2,1,0:T(8,128)} %get-tuple-element.33, f32[8,512]{1,0:T(8,128)S(1)} %get-tuple-element.32), kind=kLoop, calls=%fused_computation.15 | loop fusion | flops 16777216 | bytes 50348032 | tf_op jit(solution)/shard_map/convert_element_type | solution.py:53
  109.6 13.0 %multiply_reduce_fusion.2 = (f32[512,8]{0,1:T(8,128)}, bf16[8,64,512]{2,1,0:T(8,128)(2,1)}) fusion(bf16[512,512]{0,1:T(8,128)(2,1)S(1)} %convolution_convert_fusion.1, bf16[2048,8,64]{0,2,1:T(8,128)(2,1)} %bitcast.73, bf16[8,512,2048]{2,1,0:T(8,128)(2,1)} %fusion.8), kind=kOutput, calls=%fused_computation.49 | convolution fusion | flops 1075048448 | bytes 19939328 | tf_op jit(solution)/shard_map/hij,jhe->ihe/dot_general | solution.py:55
  122.6 10.8 %fusion.40 = f32[8,64,2048]{2,1,0:T(8,128)} fusion(bf16[512,8,64]{0,2,1:T(8,128)(2,1)S(1)} %bitcast.77, bf16[8,512,2048]{2,1,0:T(8,128)(2,1)} %fusion.8), kind=kOutput, calls=%fused_computation.70 | convolution fusion | flops 1073741824 | bytes 21495808 | tf_op jit(solution)/shard_map/hij,ihe->jhe/dot_general | solution.py:81
  133.4 13.4 %multiply_convert_fusion = bf16[8,512,2048]{2,1,0:T(8,128)(2,1)S(1)} fusion(bf16[512,8,64]{0,2,1:T(8,128)(2,1)S(1)} %bitcast.78, bf16[2048,8,64]{0,2,1:T(8,128)(2,1)} %bitcast.74, f32[8,512]{1,0:T(8,128)} %bitcast.85, f32[8,512,2048]{2,1,0:T(8,128)} %get-tuple-element.33, f32[8,512]{1,0:T(8,128)S(1)} %get-tuple-element.32), kind=kOutput, calls=%fused_computation.5 | convolution fusion | flops 1115684864 | bytes 52985856 | tf_op jit(solution)/shard_map/ihe,jhe->hij/dot_general | solution.py:72
  146.8 7.0 fusion.39
  153.8 7.8 pad_maximum_fusion
  161.6 0.7 copy-done.14
  162.3 0.1 reshape.105
  162.4 0.3 copy-done.1
  162.6 5.1 gather_fusion
  167.7 9.5 %all-to-all-start = ((bf16[32,32,512]{2,1,0:T(8,128)(2,1)}), bf16[32,32,512]{2,1,0:T(8,128)(2,1)}, u32[]{:S(2)}, u32[]{:S(2)}) async-start(bf16[32,32,512]{2,1,0:T(8,128)(2,1)} %bitcast.79), calls=%async_computation | async-start | bytes 2097152 | tf_op jit(solution)/shard_map/all_to_all | solution.py:28
  177.3 0.2 all-reduce.7.cloned.1.call-start
  177.5 1.1 convert_element_type.58
  178.6 0.8 copy.29
  179.4 0.1 copy.25
  179.6 0.2 reshape.113
  179.8 0.1 copy.24
  179.9 1.1 reshape.121
  181.0 1.4 fusion.38
  182.4 26.6 %all-to-all-done = bf16[32,32,512]{2,1,0:T(8,128)(2,1)} async-done(((bf16[32,32,512]{2,1,0:T(8,128)(2,1)}), bf16[32,32,512]{2,1,0:T(8,128)(2,1)}, u32[]{:S(2)}, u32[]{:S(2)}) %all-to-all-start) | async-done | bytes 1048608 | tf_op jit(solution)/shard_map/all_to_all | solution.py:28
  209.0 6.1 fusion.26
  215.1 25.3 %gather_fusion.1 = f32[4096,1024]{1,0:T(8,128)} fusion(f32[1536,1024]{1,0:T(8,128)} %fusion.26, s32[4096]{0:T(1024)S(1)} %broadcast_clamp_fusion), kind=kCustom, calls=%fused_computation.1 | custom fusion | bytes 33570816 | tf_op jit(solution)/shard_map/gather | solution.py:33
  240.4 19.1 %fusion.34 = (bf16[512,512]{1,0:T(8,128)(2,1)S(1)}, f32[512,8,512]{2,1,0:T(8,128)}, f32[512,8,512]{2,1,0:T(8,128)}, f32[512,512]{1,0:T(8,128)}) fusion(f32[512,8,1024]{2,1,0:T(8,128)} %bitcast.68, f32[512,512]{1,0:T(8,128)} %fusion.38, f32[512,512]{1,0:T(8,128)} %convert_element_type.58, f32[512,8]{1,0:T(8,128)S(1)} %copy.24), kind=kLoop, calls=%fused_computation.65 | loop fusion | flops 28835840 | bytes 37240832 | tf_op jit(solution)/shard_map/reduce_sum | solution.py:96
  259.5 38.4 %scatter_custom_fusion = f32[1536,1024]{1,0:T(8,128)} fusion(s32[4096]{0:T(1024)S(1)} %reshape.121, f32[512,8,512]{2,1,0:T(8,128)} %get-tuple-element.28, f32[]{:T(128)} %constant.2.clone.1, f32[512,8,512]{2,1,0:T(8,128)} %get-tuple-element.27, f32[]{:T(128)} %constant.7.clone.1), kind=kCustom, calls=%fused_computation.10 | custom fusion | flops 8388608 | bytes 23068680 | tf_op jit(solution)/shard_map/scatter-add | solution.py:98
  298.0 1.5 convolution_bitcast_fusion.1
  299.4 6.2 fusion.20
  305.7 1.4 fusion.41
  307.1 12.4 %convolution_convert_fusion.2 = bf16[8,64,512]{2,1,0:T(8,128)(2,1)} fusion(bf16[2048,8,64]{0,2,1:T(8,128)(2,1)} %bitcast.72, bf16[8,512,2048]{2,1,0:T(8,128)(2,1)} %copy-done.2), kind=kOutput, calls=%fused_computation.47 | convolution fusion | flops 1074003968 | bytes 19398656 | tf_op jit(solution)/shard_map/hij,jhe->ihe/dot_general | solution.py:76
  319.5 1.7 convert.13
  321.2 1.0 copy-done.10
  322.2 3.7 convolution_bitcast_fusion
  325.9 0.0 all-reduce.5.cloned.1.call-start
  326.0 137.5 %all-reduce.7.cloned.1.call-done = (f32[512,512]{0,1:T(8,128)}, f32[512,1024]{1,0:T(8,128)}, f32[512,1536]{0,1:T(8,128)}, f32[512,512]{1,0:T(8,128)}) async-done(((f32[512,512]{0,1:T(8,128)}, f32[512,1024]{1,0:T(8,128)}, f32[512,1536]{0,1:T(8,128)}, f32[512,512]{1,0:T(8,128)}), (f32[512,512]{0,1:T(8,128)}, f32[512,1024]{1,0:T(8,128)}, f32[512,1536]{0,1:T(8,128)}, ...) | async-done | bytes 7340048 | tf_op jit(solution)/shard_map/psum | solution.py:119
  463.5 4.9 fusion.22
  468.4 1.7 copy-done.12
  470.1 1.1 slice.64
  471.2 9.8 %all-to-all-start.1 = ((bf16[32,32,512]{2,1,0:T(8,128)(2,1)}), bf16[32,32,512]{2,1,0:T(8,128)(2,1)}, u32[]{:S(2)}, u32[]{:S(2)}) async-start(bf16[32,32,512]{2,1,0:T(8,128)(2,1)} %bitcast.80), calls=%async_computation.2 | async-start | bytes 2097152 | tf_op jit(solution)/shard_map/all_to_all | solution.py:104
  480.9 0.1 reshape.129
  481.0 2.9 fusion.25
  483.9 2.7 fusion.24
  486.6 1.4 convolution_add_fusion
  488.1 24.6 %all-to-all-done.1 = bf16[32,32,512]{2,1,0:T(8,128)(2,1)} async-done(((bf16[32,32,512]{2,1,0:T(8,128)(2,1)}), bf16[32,32,512]{2,1,0:T(8,128)(2,1)}, u32[]{:S(2)}, u32[]{:S(2)}) %all-to-all-start.1) | async-done | bytes 1048608 | tf_op jit(solution)/shard_map/all_to_all | solution.py:104
  512.7 9.4 %scatter_custom_fusion.1 = f32[512,512]{1,0:T(8,128)} fusion(f32[512,512]{1,0:T(8,128)} %convolution_add_fusion, s32[1024]{0:T(1024)S(1)} %reshape.129, bf16[1024,512]{1,0:T(8,128)(2,1)} %bitcast.26), kind=kCustom, calls=%fused_computation.32 | custom fusion | flops 1048576 | bytes 2097152 | tf_op jit(solution)/shard_map/scatter-add | solution.py:111
  522.1 2.1 convert_element_type.66
  524.1 360.3 %all-reduce.5.cloned.1.call-done = (f32[512,512]{0,1:T(8,128)}, f32[512,1024]{1,0:T(8,128)}, f32[512,1536]{0,1:T(8,128)}, f32[512,512]{1,0:T(8,128)}) async-done(((f32[512,512]{0,1:T(8,128)}, f32[512,1024]{1,0:T(8,128)}, f32[512,1536]{0,1:T(8,128)}, f32[512,512]{1,0:T(8,128)}), (f32[512,512]{0,1:T(8,128)}, f32[512,1024]{1,0:T(8,128)}, f32[512,1536]{0,1:T(8,128)}, ...) | async-done | bytes 7340048 | tf_op jit(solution)/shard_map/psum | solution.py:118
  884.4 2.6 copy.30
  887.0 3.5 copy.31
  890.6 3.2 copy.41
  893.7 1.0 copy.42
  (37 shorter events, 0.2 us)
Async XLA Ops:
  7.2 1.4 copy-start
  7.2 7.8 copy-start.3
  7.2 7.8 copy-start.5
  7.2 54.3 %all-gather.2.cloned.1.call-start = ((), (), s32[]{:S(2)}) async-start(), calls=%async_computation.3 | async-start | bytes 5242880 | tf_op jit(solution)/shard_map/all_gather | solution.py:41
  10.6 1.1 copy-start.9
  12.9 306.6 %reduce-scatter.2.cloned.1.call-start = ((), (), s32[]{:S(2)}) async-start(), calls=%async_computation.4 | async-start | bytes 10485760 | tf_op jit(solution)/shard_map/reduce_scatter | solution.py:82
  66.0 7.9 copy-start.8
  146.8 7.0 copy-start.2
  161.6 0.7 copy-start.14
  161.6 1.1 copy-start.1
  162.6 15.9 %copy-start.13 = (s32[512,8]{0,1:T(8,128)S(1)}, s32[512,8]{0,1:T(8,128)}, u32[]{:S(2)}) copy-start(s32[512,8]{0,1:T(8,128)} %param.11) | copy-start | bytes 49156
  162.6 17.1 %copy-start.15 = (s32[512,8]{0,1:T(8,128)S(1)}, s32[512,8]{0,1:T(8,128)}, u32[]{:S(2)}) copy-start(s32[512,8]{0,1:T(8,128)} %param.12) | copy-start | bytes 49156
  162.6 18.4 %copy-start.6 = (bf16[512,512]{1,0:T(8,128)(2,1)S(1)}, bf16[512,512]{1,0:T(8,128)(2,1)}, u32[]{:S(2)}) copy-start(bf16[512,512]{1,0:T(8,128)(2,1)} %param.13) | copy-start | bytes 1572868
  167.7 41.3 %all-to-all-start = ((bf16[32,32,512]{2,1,0:T(8,128)(2,1)}), bf16[32,32,512]{2,1,0:T(8,128)(2,1)}, u32[]{:S(2)}, u32[]{:S(2)}) async-start(bf16[32,32,512]{2,1,0:T(8,128)(2,1)} %bitcast.79), calls=%async_computation | async-start | bytes 2097152 | tf_op jit(solution)/shard_map/all_to_all | solution.py:28
  177.3 286.2 %all-reduce.7.cloned.1.call-start = ((), (), s32[]{:S(2)}) async-start(), calls=%async_computation.6 | async-start | bytes 14680064 | tf_op jit(solution)/shard_map/psum | solution.py:119
  297.9 7.7 copy-start.4
  321.2 1.0 copy-start.10
  325.9 558.5 %all-reduce.5.cloned.1.call-start = ((), (), s32[]{:S(2)}) async-start(), calls=%async_computation.5 | async-start | bytes 14680064 | tf_op jit(solution)/shard_map/psum | solution.py:118
  468.4 1.7 copy-start.12
  471.2 41.5 %all-to-all-start.1 = ((bf16[32,32,512]{2,1,0:T(8,128)(2,1)}), bf16[32,32,512]{2,1,0:T(8,128)(2,1)}, u32[]{:S(2)}, u32[]{:S(2)}) async-start(bf16[32,32,512]{2,1,0:T(8,128)(2,1)} %bitcast.80), calls=%async_computation.2 | async-start | bytes 2097152 | tf_op jit(solution)/shard_map/all_to_all | solution.py:104
  481.0 5.6 copy-start.7
  884.4 9.3 %copy-start.11 = (f32[512,512]{1,0:T(8,128)S(1)}, f32[512,512]{1,0:T(8,128)}, u32[]{:S(2)}) copy-start(f32[512,512]{1,0:T(8,128)} %get-tuple-element.41) | copy-start | bytes 3145732
Sparse Core Ops, SparseCore 0:
  13.0 48.4 all-gather.1
  161.7 91.6 reduce-scatter.1
  326.0 137.3 all-reduce.6
  466.1 418.2 all-reduce.4
